TPU v7x, 1024 devices: a whole 4x4x32 slice. The times are simulated.
1024 devices in a mesh: wide: 32 (over z), narrow: 32 (over y, x, core).
Axes of the slice: x: 4, y: 4, z: 32, core: 2. Of those that a mesh axis runs over, the one named last changes fastest.
Arguments:
- tokens: bfloat16 [131072, 3584], P(('wide', 'narrow')), may hold values from -6 to 6
- cotangent: bfloat16 [131072, 3584], P(('wide', 'narrow')), may hold values from -6 to 6
- expert_ids: int32 [131072, 8], P(('wide', 'narrow')), may hold values from 0 to 383, as said below
- slots: int32 [131072, 8], P(('wide', 'narrow')), may hold values from 0 to 2, as said below
- probs: bfloat16 [131072, 8], P(('wide', 'narrow')), may hold values from 0.049804688 to 1
- w_gate: bfloat16 [3584, 8192], P('wide', 'narrow'), may hold values from -0.09375 to 0.09375
- w_up: bfloat16 [3584, 8192], P('wide', 'narrow'), may hold values from -0.09375 to 0.09375
- w_down: bfloat16 [8192, 3584], P('narrow', 'wide'), may hold values from -0.125 to 0.125
Outputs:
- token_grad: bfloat16 [131072, 3584], P(('wide', 'narrow'))
- prob_grad: float32 [131072, 8], P(('wide', 'narrow'))
Inputs may be any that keep to these rules, and one draw needn't show every extreme that they name: `expert_ids`: each row names 8 different experts. Within the 128 rows of one device every expert below 4 is named by 1 to 3 rows, and in each group of 4096 tokens one such expert is named by exactly 3 rows on every device. Within the rows of one device, the choices that name one expert below 4 hold distinct slots.
All inputs are finite; a program needn't handle non-finite values.
Results may differ from a plain program's by a relative error of at most 0.019.
Values may be sent and summed in bfloat16 or wider, within the bound.
A program may use at most 32 MiB of HBM per device.

v0:
```python
import jax
import jax.numpy as jnp
from jax import lax
from jax.sharding import PartitionSpec as P

GROUP = 8
CAP = 3


def silu_parts(values):
    sigma = jax.nn.sigmoid(values)
    return (values * sigma, sigma * (1.0 + values * (1.0 - sigma)))


def contract_last(left, right):
    return lax.dot_general(
        left, right, (((1,), (1,)), ((), ())), preferred_element_type=jnp.float32
    )


def shards(tokens, cotangent, expert_ids, slots, probs, w_gate, w_up, w_down):
    narrow_count = lax.axis_size("narrow")
    experts_here = narrow_count // GROUP
    tok_count = tokens.shape[0]
    model_width = tokens.shape[1]
    lanes = experts_here * CAP
    slot_count = narrow_count * CAP
    inside = expert_ids < experts_here
    target = jnp.where(inside, expert_ids * CAP + slots, lanes)
    owner_row = jnp.broadcast_to(jnp.arange(tok_count, dtype=jnp.int32)[:, None], target.shape)
    prob_wide = probs.astype(jnp.float32)
    source = (
        jnp.full((lanes,), tok_count, jnp.int32)
        .at[target.reshape(-1)]
        .set(owner_row.reshape(-1), mode="drop")
    )
    row_scale = (
        jnp.zeros((lanes,), jnp.float32)
        .at[target.reshape(-1)]
        .set(prob_wide.reshape(-1), mode="drop")
    )
    zero_row = jnp.zeros((1, model_width), jnp.bfloat16)
    padded_x = jnp.concatenate([tokens, zero_row], 0)
    padded_dy = jnp.concatenate([cotangent, zero_row], 0)
    pick_x = padded_x[source]
    pick_d = (row_scale[:, None] * padded_dy[source].astype(jnp.float32)).astype(jnp.bfloat16)

    def fan_blocks(rows):
        spread = jnp.broadcast_to(
            rows.reshape(experts_here, 1, CAP, model_width), (experts_here, GROUP, CAP, model_width)
        )
        return spread.reshape(narrow_count, CAP, model_width)

    got_x, got_d = (
        lax.all_to_all(fan_blocks(pick_x), "narrow", split_axis=0, concat_axis=0, tiled=True),
        lax.all_to_all(fan_blocks(pick_d), "narrow", split_axis=0, concat_axis=0, tiled=True),
    )
    rows_x = got_x.reshape(slot_count, model_width)
    rows_d = got_d.reshape(slot_count, model_width)
    gate_full, up_full, down_cols = (
        lax.all_gather(w_gate, "wide", axis=0, tiled=True),
        lax.all_gather(w_up, "wide", axis=0, tiled=True),
        lax.all_gather(w_down, "wide", axis=1, tiled=True),
    )
    gate_act = jnp.dot(rows_x, gate_full, preferred_element_type=jnp.float32)
    up_act = jnp.dot(rows_x, up_full, preferred_element_type=jnp.float32)
    act, slope = silu_parts(gate_act)
    hidden = (act * up_act).astype(jnp.bfloat16)
    part_out = jnp.dot(hidden, down_cols, preferred_element_type=jnp.float32).astype(jnp.bfloat16)
    d_hidden = contract_last(rows_d, down_cols)
    d_gate = (d_hidden * up_act * slope).astype(jnp.bfloat16)
    d_up = (d_hidden * act).astype(jnp.bfloat16)
    part_dx = (contract_last(d_gate, gate_full) + contract_last(d_up, up_full)).astype(jnp.bfloat16)
    back_out, back_dx = (
        lax.all_to_all(
            part_out.reshape(narrow_count, CAP, model_width),
            "narrow",
            split_axis=0,
            concat_axis=0,
            tiled=True,
        ),
        lax.all_to_all(
            part_dx.reshape(narrow_count, CAP, model_width),
            "narrow",
            split_axis=0,
            concat_axis=0,
            tiled=True,
        ),
    )
    out_sum = jnp.sum(
        back_out.reshape(experts_here, GROUP, CAP, model_width).astype(jnp.float32), 1
    ).reshape(lanes, model_width)
    dx_sum = jnp.sum(
        back_dx.reshape(experts_here, GROUP, CAP, model_width).astype(jnp.float32), 1
    ).reshape(lanes, model_width)
    lane_ids = jnp.arange(lanes, dtype=jnp.int32)
    matches = target[:, :, None] == lane_ids[None, None, :]
    picked = jnp.sum(jnp.where(matches, 1.0, 0.0), 1)
    grad_rows = jnp.dot(
        picked, dx_sum, precision=lax.Precision.HIGHEST, preferred_element_type=jnp.float32
    )
    scores = lax.dot_general(
        cotangent.astype(jnp.float32),
        out_sum,
        (((1,), (1,)), ((), ())),
        precision=lax.Precision.HIGHEST,
        preferred_element_type=jnp.float32,
    )
    prob_grad = jnp.where(
        inside, jnp.take_along_axis(scores, jnp.minimum(target, lanes - 1), 1), 0.0
    )
    return (grad_rows.astype(jnp.bfloat16), prob_grad)


def solution(mesh):
    in_specs = (
        P(("wide", "narrow"), None),
        P(("wide", "narrow"), None),
        P(("wide", "narrow"), None),
        P(("wide", "narrow"), None),
        P(("wide", "narrow"), None),
        P("wide", "narrow"),
        P("wide", "narrow"),
        P("narrow", "wide"),
    )
    out_specs = (P(("wide", "narrow"), None), P(("wide", "narrow"), None))
    return jax.shard_map(shards, mesh=mesh, in_specs=in_specs, out_specs=out_specs, check_vma=False)
```

profile of v0, /device:TPU:1, one launch (start us, length us, event | category | flops | bytes accessed | tf_op | source)
XLA Modules:
  0.0 488.4 jit_solution(10206500882759651241)
XLA Ops:
  7.2 0.7 all-gather.8.cloned.1.call-update
  8.0 0.7 all-gather.6.cloned.1.call-update
  8.7 0.7 all-gather.4.cloned.1.call-update
  9.4 0.7 bitcast_or_fusion
  10.1 0.1 copy.24
  10.2 0.1 reshape.105
  10.3 0.1 reshape.157
  10.4 1.2 concatenate.6
  11.7 4.3 scatter_custom_fusion.1
  16.0 0.6 gather_fusion
  16.6 0.1 reshape.120
  16.7 0.1 copy.25
  16.9 0.1 reshape.149
  16.9 4.3 scatter_custom_fusion
  21.3 0.1 multiply_convert_fusion
  21.5 1.2 broadcast_in_dim.53
  22.6 17.7 %all-to-all-start = ((bf16[32,3,3584]{2,1,0:T(4,128)(2,1)}), bf16[32,3,3584]{2,1,0:T(4,128)(2,1)S(1)}, u32[]{:S(2)}, u32[]{:S(2)}) async-start(bf16[32,3,3584]{2,1,0:T(4,128)(2,1)} %bitcast.1), calls=%async_computation | async-start | bytes 1835008 | tf_op jit(solution)/shard_map/all_to_all | solution.py:56
  40.4 0.6 gather_fusion.1
  41.1 15.1 %all-to-all-done = bf16[32,3,3584]{2,1,0:T(4,128)(2,1)S(1)} async-done(((bf16[32,3,3584]{2,1,0:T(4,128)(2,1)}), bf16[32,3,3584]{2,1,0:T(4,128)(2,1)S(1)}, u32[]{:S(2)}, u32[]{:S(2)}) %all-to-all-start) | async-done | bytes 688160 | tf_op jit(solution)/shard_map/all_to_all | solution.py:56
  56.2 1.2 broadcast_in_dim.55
  57.4 4.0 all-to-all-start.1
  61.4 0.6 reshape.110
  62.0 15.3 %all-to-all-done.1 = bf16[32,3,3584]{2,1,0:T(4,128)(2,1)S(1)} async-done(((bf16[32,3,3584]{2,1,0:T(4,128)(2,1)}), bf16[32,3,3584]{2,1,0:T(4,128)(2,1)S(1)}, u32[]{:S(2)}, u32[]{:S(2)}) %all-to-all-start.1) | async-done | bytes 688160 | tf_op jit(solution)/shard_map/all_to_all | solution.py:55
  77.2 0.6 reshape.112
  77.8 59.3 %all-gather.8.cloned.1.call-done = bf16[3584,256]{1,0:T(8,128)(2,1)} async-done(((bf16[112,256]{1,0:T(8,128)(2,1)}), bf16[3584,256]{1,0:T(8,128)(2,1)}) %all-gather.8.cloned.1.call-update) | async-done | bytes 1835024 | tf_op jit(solution)/shard_map/all_gather | solution.py:61
  137.1 1.9 fusion.15
  139.0 130.6 %all-gather.6.cloned.1.call-done = bf16[3584,256]{1,0:T(8,128)(2,1)} async-done(((bf16[112,256]{1,0:T(8,128)(2,1)}), bf16[3584,256]{1,0:T(8,128)(2,1)}) %all-gather.6.cloned.1.call-update) | async-done | bytes 1835024 | tf_op jit(solution)/shard_map/all_gather | solution.py:62
  269.7 1.9 fusion.14
  271.6 130.1 %all-gather.4.cloned.1.call-done = bf16[256,3584]{0,1:T(8,128)(2,1)} async-done(((bf16[256,112]{0,1:T(8,128)(2,1)}), bf16[256,3584]{0,1:T(8,128)(2,1)}) %all-gather.4.cloned.1.call-update) | async-done | bytes 1835024 | tf_op jit(solution)/shard_map/all_gather | solution.py:63
  401.7 1.9 fusion.13
  403.7 0.7 fusion.2
  404.4 0.8 copy-done.2
  405.2 0.7 fusion
  405.9 1.2 reshape.113
  407.1 27.5 %all-to-all-start.2 = ((bf16[32,3,3584]{2,1,0:T(4,128)(2,1)}), bf16[32,3,3584]{2,1,0:T(4,128)(2,1)S(1)}, u32[]{:S(2)}, u32[]{:S(2)}) async-start(bf16[32,3,3584]{2,1,0:T(4,128)(2,1)} %reshape.113), calls=%async_computation.2 | async-start | bytes 1835008 | tf_op jit(solution)/shard_map/all_to_all | solution.py:82
  434.6 1.6 convolution_convert_fusion.1
  436.2 1.2 reshape.115
  437.3 13.0 %all-to-all-done.2 = bf16[32,3,3584]{2,1,0:T(4,128)(2,1)S(1)} async-done(((bf16[32,3,3584]{2,1,0:T(4,128)(2,1)}), bf16[32,3,3584]{2,1,0:T(4,128)(2,1)S(1)}, u32[]{:S(2)}, u32[]{:S(2)}) %all-to-all-start.2) | async-done | bytes 688160 | tf_op jit(solution)/shard_map/all_to_all | solution.py:82
  450.3 4.0 all-to-all-start.3
  454.3 0.1 copy.26
  454.4 0.1 reshape.139
  454.5 0.4 convert_reduce_fusion.1
  455.0 15.1 %all-to-all-done.3 = bf16[32,3,3584]{2,1,0:T(4,128)(2,1)S(1)} async-done(((bf16[32,3,3584]{2,1,0:T(4,128)(2,1)}), bf16[32,3,3584]{2,1,0:T(4,128)(2,1)S(1)}, u32[]{:S(2)}, u32[]{:S(2)}) %all-to-all-start.3) | async-done | bytes 688160 | tf_op jit(solution)/shard_map/all_to_all | solution.py:75
  470.2 0.4 convert_reduce_fusion
  470.7 0.8 convolution_bitcast_fusion
  471.5 7.0 %gather_fusion.2 = f32[1024]{0:T(1024)S(1)} fusion(f32[128,12]{0,1:T(8,128)S(1)} %convolution_bitcast_fusion, s32[1024]{0:T(1024)S(1)} %reshape.139), kind=kCustom, calls=%fused_computation.2 | custom fusion | bytes 16384 | tf_op jit(solution)/shard_map/jit(take_along_axis)/gather | solution.py:110
  478.7 0.6 select_select_fusion
  479.3 2.6 convolution_convert_fusion
  (30 shorter events, 0.7 us)
Async XLA Ops:
  7.2 129.9 %all-gather.8.cloned.1.call-start = ((), (), s32[]{:S(2)}) async-start(), calls=%async_computation.6 | async-start | bytes 1892352 | tf_op jit(solution)/shard_map/all_gather | solution.py:61
  7.9 8.8 %copy-start.7 = (bf16[128,8]{0,1:T(8,128)(2,1)S(1)}, bf16[128,8]{0,1:T(8,128)(2,1)}, u32[]{:S(2)}) copy-start(bf16[128,8]{0,1:T(8,128)(2,1)} %param.12) | copy-start | bytes 6148
  7.9 261.8 %all-gather.6.cloned.1.call-start = ((), (), s32[]{:S(2)}) async-start(), calls=%async_computation.5 | async-start | bytes 1892352 | tf_op jit(solution)/shard_map/all_gather | solution.py:62
  8.7 393.1 %all-gather.4.cloned.1.call-start = ((), (), s32[]{:S(2)}) async-start(), calls=%async_computation.4 | async-start | bytes 1892352 | tf_op jit(solution)/shard_map/all_gather | solution.py:63
  16.6 23.7 %copy-start.4 = (bf16[128,3584]{1,0:T(8,128)(2,1)S(1)}, bf16[128,3584]{1,0:T(8,128)(2,1)}, u32[]{:S(2)}) copy-start(bf16[128,3584]{1,0:T(8,128)(2,1)} %param.8) | copy-start | bytes 2752516
  22.6 33.6 %all-to-all-start = ((bf16[32,3,3584]{2,1,0:T(4,128)(2,1)}), bf16[32,3,3584]{2,1,0:T(4,128)(2,1)S(1)}, u32[]{:S(2)}, u32[]{:S(2)}) async-start(bf16[32,3,3584]{2,1,0:T(4,128)(2,1)} %bitcast.1), calls=%async_computation | async-start | bytes 1835008 | tf_op jit(solution)/shard_map/all_to_all | solution.py:56
  57.4 19.9 %all-to-all-start.1 = ((bf16[32,3,3584]{2,1,0:T(4,128)(2,1)}), bf16[32,3,3584]{2,1,0:T(4,128)(2,1)S(1)}, u32[]{:S(2)}, u32[]{:S(2)}) async-start(bf16[32,3,3584]{2,1,0:T(4,128)(2,1)} %bitcast.2), calls=%async_computation.1 | async-start | bytes 1835008 | tf_op jit(solution)/shard_map/all_to_all | solution.py:55
  271.6 132.8 %copy-start.5 = (f32[96,256]{1,0:T(8,128)}, f32[96,256]{1,0:T(8,128)S(1)}, u32[]{:S(2)}) copy-start(f32[96,256]{1,0:T(8,128)S(1)} %fusion.14) | copy-start | bytes 294916
  271.6 132.1 %copy-start = (bf16[3584,256]{1,0:T(8,128)(2,1)S(1)}, bf16[3584,256]{1,0:T(8,128)(2,1)}, u32[]{:S(2)}) copy-start(bf16[3584,256]{1,0:T(8,128)(2,1)} %all-gather.8.cloned.1.call-done) | copy-start | bytes 5505028
  403.7 1.5 copy-start.2
  405.9 28.7 %copy-start.1 = (bf16[256,3584]{0,1:T(8,128)(2,1)S(1)}, bf16[256,3584]{0,1:T(8,128)(2,1)}, u32[]{:S(2)}) copy-start(bf16[256,3584]{0,1:T(8,128)(2,1)} %all-gather.4.cloned.1.call-done) | copy-start | bytes 5505028
  407.1 43.3 %all-to-all-start.2 = ((bf16[32,3,3584]{2,1,0:T(4,128)(2,1)}), bf16[32,3,3584]{2,1,0:T(4,128)(2,1)S(1)}, u32[]{:S(2)}, u32[]{:S(2)}) async-start(bf16[32,3,3584]{2,1,0:T(4,128)(2,1)} %reshape.113), calls=%async_computation.2 | async-start | bytes 1835008 | tf_op jit(solution)/shard_map/all_to_all | solution.py:82
  450.3 19.9 %all-to-all-start.3 = ((bf16[32,3,3584]{2,1,0:T(4,128)(2,1)}), bf16[32,3,3584]{2,1,0:T(4,128)(2,1)S(1)}, u32[]{:S(2)}, u32[]{:S(2)}) async-start(bf16[32,3,3584]{2,1,0:T(4,128)(2,1)} %reshape.115), calls=%async_computation.3 | async-start | bytes 1835008 | tf_op jit(solution)/shard_map/all_to_all | solution.py:75
  454.3 16.4 %copy-start.3 = (bf16[128,3584]{1,0:T(8,128)(2,1)S(1)}, bf16[128,3584]{1,0:T(8,128)(2,1)}, u32[]{:S(2)}) copy-start(bf16[128,3584]{1,0:T(8,128)(2,1)} %param.9) | copy-start | bytes 2752516
  471.5 7.2 %copy-start.6 = (s32[128,8]{0,1:T(8,128)S(1)}, s32[128,8]{0,1:T(8,128)}, u32[]{:S(2)}) copy-start(s32[128,8]{0,1:T(8,128)} %param.10) | copy-start | bytes 12292
Sparse Core Ops, SparseCore 0:
  10.7 126.4 all-gather.7
  139.8 129.8 all-gather.5
  272.3 129.3 all-gather.3
where the time goes:
time: 489 us; the launch traced here: 488 us
  waiting for transfers between devices  381 us (78%)
  starting transfers between devices  53.3 us (11%)
  local copies, waits for them, and re-layouts  26.1 us (5%)
  between operations  14.1 us (3%)
  matrix products  12.1 us (2%)
    all_gather x1, waiting for transfers between devices, shards(): lax.all_gather(w_up, 'wide', axis=0, tiled=True)  131 us
    all_gather x1, waiting for transfers between devices, shards(): lax.all_gather(w_down, 'wide', axis=1, tiled=True)  130 us
    all_gather x1, waiting for transfers between devices, shards(): lax.all_gather(w_gate, 'wide', axis=0, tiled=True)  59.3 us
    all_to_all x1, starting transfers between devices, shards(): lax.all_to_all(part_dx.reshape(narrow_count, CAP, model_width), 'narrow',...  27.5 us
    all_to_all x1, starting transfers between devices, shards(): lax.all_to_all(fan_blocks(pick_d), 'narrow', split_axis=0, concat_axis=0,...  17.7 us
    all_to_all x1, waiting for transfers between devices, shards(): lax.all_to_all(fan_blocks(pick_x), 'narrow', split_axis=0, concat_axis=0,...  15.3 us
    all_to_all x1, waiting for transfers between devices, shards(): lax.all_to_all(part_out.reshape(narrow_count, CAP, model_width), 'narrow'...  15.1 us
    all_to_all x1, waiting for transfers between devices, shards(): lax.all_to_all(fan_blocks(pick_d), 'narrow', split_axis=0, concat_axis=0,...  15.1 us
  transfers between devices with their start and end apart: 7, of which 7 were waited for; matrix products, arithmetic and copies ran while one was open for 5% of the time, Pallas kernels for 0%

commit v1 on v0

v1 whole, which is shorter than its diff:
```python
import functools

import jax
import jax.numpy as jnp
from jax import lax
from jax.experimental import pallas as pl
from jax.experimental.pallas import tpu as pltpu
from jax.sharding import PartitionSpec as P

MESH = pl.DeviceIdType.MESH
F32 = jnp.float32
BF16 = jnp.bfloat16

NZ = 32
NP = 32
EXP = 4
PER_EXP = 8
TOK = 128
D = 3584
HID = 256
SH = 112
NQ = 4
QW = D // NQ
ROWS = NP * 4
HALF = NZ // 2


def place(n):
    return lax.rem(n, 2) * (NP // 2) + n // 2


def kernel(
    tok_hbm, cot_hbm, ids_ref, slots_ref, probs_ref, wg_hbm, wu_hbm, wd_ref,
    grad_ref, prob_ref,
    wbuf, tok, cot, msg, xin, xq, acc, dxs, outb, rin,
    loc_sem, ring_send, ring_recv, x_send, x_recv, r_send, r_recv,
):
    w = lax.axis_index("wide")
    n = lax.axis_index("narrow")
    right, left = lax.rem(w + 1, NZ), lax.rem(w + NZ - 1, NZ)
    my_place = place(n)
    my_exp = n // PER_EXP

    def load(i, src, dst):
        return pltpu.make_async_copy(src, dst, loc_sem.at[i])

    def rows_of(shard):
        return pl.ds(pl.multiple_of(shard * SH, 16), SH)

    loads = [
        load(0, wg_hbm, wbuf.at[0, rows_of(w)]),
        load(1, wu_hbm, wbuf.at[1, rows_of(w)]),
        load(2, tok_hbm, tok),
        load(3, cot_hbm, cot),
    ]
    for one in loads:
        one.start()

    barrier = pltpu.get_barrier_semaphore()

    def greet(d, carry):
        pl.semaphore_signal(barrier, inc=1, device_id=(w, lax.rem(n + d, NP)), device_id_type=MESH)
        return carry

    pl.semaphore_signal(barrier, inc=1, device_id=(left, n), device_id_type=MESH)
    pl.semaphore_signal(barrier, inc=1, device_id=(right, n), device_id_type=MESH)
    lax.fori_loop(1, NP, greet, 0)
    pl.semaphore_wait(barrier, NP + 1)

    def sem_at(way, k, c):
        return (way * (HALF + 1) + k) * 3 + c

    def hop(way, k, c, lo=0, size=SH, src=None):
        if way == 0:
            shard, to = lax.rem(w + NZ + 1 - k, NZ), right
        else:
            shard, to = lax.rem(w + NZ - 1 + k, NZ), left
        span = pl.ds(pl.multiple_of(shard * SH + lo, 16), size)
        here = wbuf.at[c, span]
        return pltpu.make_async_remote_copy(
            src_ref=here if src is None else src,
            dst_ref=here,
            send_sem=ring_send.at[sem_at(way, k, c)],
            recv_sem=ring_recv.at[sem_at(way, k, c)],
            device_id=(to, n),
            device_id_type=MESH,
        )

    def landed(way, k, c, lo=0, size=SH):
        shard = lax.rem(w + NZ - k, NZ) if way == 0 else lax.rem(w + k, NZ)
        here = wbuf.at[c, pl.ds(pl.multiple_of(shard * SH + lo, 16), size)]
        return pltpu.make_async_remote_copy(
            src_ref=here,
            dst_ref=here,
            send_sem=ring_send.at[sem_at(way, k, c)],
            recv_sem=ring_recv.at[sem_at(way, k, c)],
            device_id=(right, n),
            device_id_type=MESH,
        )

    for c, src in ((0, wg_hbm), (1, wu_hbm)):
        for way in (0, 1):
            hop(way, 1, c, src=src).start()
    eye = (
        lax.broadcasted_iota(jnp.int32, (SH, SH), 0) == lax.broadcasted_iota(jnp.int32, (SH, SH), 1)
    ).astype(F32).astype(BF16)
    wbuf[2, rows_of(w), :] = lax.dot_general(
        eye, wd_ref[...], (((1,), (1,)), ((), ())), preferred_element_type=F32
    ).astype(BF16)
    for way in (0, 1):
        hop(way, 1, 2).start()

    ids = ids_ref[...]
    target = jnp.where(ids < EXP, ids * 4 + slots_ref[...], -1)
    lane = lax.broadcasted_iota(jnp.int32, (TOK, 128), 1)
    code = jnp.where(lane < 64, (lane // 16) * 4 + lax.rem(lane, 4), -2)
    picks = jnp.zeros((TOK, 128), F32)
    for k in range(8):
        picks = picks + jnp.where(target[:, k : k + 1] == code, 1.0, 0.0)
    picks = jnp.transpose(picks)[:64].astype(BF16)
    row_q = lax.rem(lax.broadcasted_iota(jnp.int32, (64, QW), 0) // 4, NQ)
    loads[2].wait()
    loads[3].wait()
    for a, src in ((0, tok), (1, cot)):
        rows = jnp.zeros((64, QW), F32)
        for q in range(NQ):
            part = jnp.dot(picks, src[:, q * QW : (q + 1) * QW], preferred_element_type=F32)
            rows = jnp.where(row_q == q, part, rows)
        for e in range(EXP):
            msg[e, a] = rows[e * 16 : (e + 1) * 16].astype(BF16)

    def x_copy(d):
        dest = lax.rem(n + d, NP)
        return pltpu.make_async_remote_copy(
            src_ref=msg.at[dest // PER_EXP],
            dst_ref=xin.at[:, my_place],
            send_sem=x_send.at[d],
            recv_sem=x_recv.at[my_place],
            device_id=(w, dest),
            device_id_type=MESH,
        )

    def x_landed(d):
        origin = place(lax.rem(n + d, NP))
        return pltpu.make_async_remote_copy(
            src_ref=msg.at[0],
            dst_ref=xin.at[:, origin],
            send_sem=x_send.at[d],
            recv_sem=x_recv.at[origin],
            device_id=(w, n),
            device_id_type=MESH,
        )

    def x_start(d, carry):
        x_copy(d).start()
        return carry

    lax.fori_loop(1, NP, x_start, 0)
    own_x = load(4, msg.at[my_exp], xin.at[:, my_place])
    own_x.start()
    acc[...] = jnp.zeros_like(acc)
    own_x.wait()
    loads[0].wait()
    loads[1].wait()

    def step(k):
        for c in range(3):
            for way in (0, 1):
                landed(way, k, c).wait_recv()
                hop(way, k + 1, c).start()

    def steps(lo, hi, more=None):
        def body(k, carry):
            step(k)
            if more is not None:
                more(k)
            return carry

        lax.fori_loop(lo, hi, body, 0)

    steps(1, 8)

    def x_wait(d, carry):
        x_landed(d).wait_recv()
        return carry

    lax.fori_loop(1, NP, x_wait, 0)

    low = lax.broadcasted_iota(jnp.int32, (8, QW), 0) < 4

    def sort_rows(unit):
        a, g = unit // 8, lax.rem(unit, 8)
        block = [xin[a, 4 * g + i].astype(F32) for i in range(4)]
        for half in range(2):
            v = [one[half * 8 : half * 8 + 8] for one in block]
            r = [pltpu.roll(one, 4, 0) for one in v]
            even = [jnp.where(low, v[0], r[1]), jnp.where(low, v[2], r[3])]
            odd = [jnp.where(low, r[0], v[1]), jnp.where(low, r[2], v[3])]
            span = pl.ds(pl.multiple_of(g * 16, 16), 16)
            xq[a, 2 * half, span, :] = jnp.concatenate(even, 0).astype(BF16)
            xq[a, 2 * half + 1, span, :] = jnp.concatenate(odd, 0).astype(BF16)

    def sort_some(k):
        for i in range(4):
            sort_rows((k - 8) * 4 + i)

    steps(8, 12, sort_some)

    def group(j):
        span = pl.ds(pl.multiple_of(j * QW, 16), QW)
        for c in range(3):
            acc[c] += jnp.dot(xq[c // 2, j], wbuf[c, span, :], preferred_element_type=F32)

    j, r = w // 8, lax.rem(w, 8)
    near = lax.rem(j + jnp.where(r <= 3, 3, 1), 4)
    far = lax.rem(j + jnp.where(r <= 3, 1, 3), 4)
    group(j)
    steps(12, 13)
    group(near)
    steps(13, 15)
    last = ((0, 0, 0, SH), (1, 1, 0, SH), (0, 2, 0, 64), (1, 2, 64, 48))
    for c in range(3):
        for way in (0, 1):
            landed(way, HALF - 1, c).wait_recv()
            for way_l, c_l, lo, size in last:
                if (way_l, c_l) == (way, c):
                    hop(way, HALF, c, lo, size).start()
    group(far)
    for way, c, lo, size in last:
        landed(way, HALF, c, lo, size).wait_recv()
    group(lax.rem(j + 2, 4))

    gate, up, raw = acc[0], acc[1], acc[2]
    sigma = 1.0 / (1.0 + jnp.exp(-gate))
    act = gate * sigma
    slope = sigma * (1.0 + gate * (1.0 - sigma))
    d_gate = (raw * up * slope).astype(BF16)
    d_up = (raw * act).astype(BF16)
    score = jnp.sum(act * up * raw, axis=1, keepdims=True)

    row = lax.broadcasted_iota(jnp.int32, (ROWS, 128), 0)
    col = lax.broadcasted_iota(jnp.int32, (ROWS, 128), 1)
    slot = lax.rem(row, 4)
    high = score.astype(BF16).astype(F32)
    marks = jnp.where(col == slot, high, 0.0) + jnp.where(col == slot + 8, score - high, 0.0)
    marks = marks + pltpu.roll(marks, 1, 0)
    marks = marks + pltpu.roll(marks, 2, 0)
    marks = jnp.where(slot == 3, marks, 0.0)

    nt = (((1,), (1,)), ((), ()))
    for q in range(NQ):
        span = pl.ds(q * QW, QW)
        dxs[q] = lax.dot_general(d_gate, wbuf[0, span, :], nt, preferred_element_type=F32) + lax.dot_general(
            d_up, wbuf[1, span, :], nt, preferred_element_type=F32
        )
    dxs[0, :, 0:128] += marks

    def pack_rows(g, carry):
        for i in range(2):
            span = pl.ds(pl.multiple_of(g * 16 + i * 8, 8), 8)
            v = [dxs[q, span, :] for q in range(NQ)]
            r = [pltpu.roll(one, 4, 0) for one in v]
            first = [jnp.where(low, v[0], r[1]), jnp.where(low, v[2], r[3])]
            second = [jnp.where(low, r[0], v[1]), jnp.where(low, r[2], v[3])]
            outb[4 * g + 2 * i] = jnp.concatenate(first, 0).astype(BF16)
            outb[4 * g + 2 * i + 1] = jnp.concatenate(second, 0).astype(BF16)
        return carry

    lax.fori_loop(0, NP // 4, pack_rows, 0)

    def r_copy(d):
        dest = lax.rem(n + d, NP)
        return pltpu.make_async_remote_copy(
            src_ref=outb.at[place(dest)],
            dst_ref=rin.at[my_place],
            send_sem=r_send.at[d],
            recv_sem=r_recv.at[my_place],
            device_id=(w, dest),
            device_id_type=MESH,
        )

    def r_landed(d):
        origin = place(lax.rem(n + d, NP))
        return pltpu.make_async_remote_copy(
            src_ref=outb.at[0],
            dst_ref=rin.at[origin],
            send_sem=r_send.at[d],
            recv_sem=r_recv.at[origin],
            device_id=(w, n),
            device_id_type=MESH,
        )

    def r_start(d, carry):
        r_copy(d).start()
        return carry

    lax.fori_loop(1, NP, r_start, 0)
    own_r = load(5, outb.at[my_place], rin.at[my_place])
    own_r.start()

    lanes = NP * 16
    lane = lax.broadcasted_iota(jnp.int32, (TOK, lanes), 1)
    code = (lax.rem(lane // 16, NP // 2) // 4) * 4 + lax.rem(lane, 4)
    lane_q = lax.rem(lane // 4, NQ)
    probs = probs_ref[...].astype(F32)
    spread = jnp.zeros((TOK, lanes), F32)
    for k in range(8):
        spread = spread + jnp.where(target[:, k : k + 1] == code, probs[:, k : k + 1], 0.0)
    own_r.wait()

    def r_wait(d, carry):
        r_landed(d).wait_recv()
        return carry

    lax.fori_loop(1, NP, r_wait, 0)
    for q in range(NQ):
        mix = jnp.where(lane_q == q, spread, 0.0).astype(BF16)
        total = jnp.zeros((TOK, QW), F32)
        total = jnp.dot(mix, rin[...].reshape(lanes, QW), preferred_element_type=F32)
        grad_ref[:, q * QW : (q + 1) * QW] = total.astype(BF16)

    s_row = lax.broadcasted_iota(jnp.int32, (16, lanes), 0)
    s_col = lax.broadcasted_iota(jnp.int32, (16, lanes), 1)
    take = (lax.rem(s_col, 16) == 3) & (lax.rem(s_col // 16, NP // 2) // 4 == s_row)
    sums = jnp.dot(
        jnp.where(take, 1.0, 0.0).astype(BF16),
        rin[:, :, 0:128].reshape(lanes, 128),
        preferred_element_type=F32,
    )
    result = jnp.zeros((TOK, 8), F32)
    for e in range(EXP):
        for s in range(3):
            value = sums[e : e + 1, s : s + 1] + sums[e : e + 1, s + 8 : s + 9]
            result = jnp.where(target == e * 4 + s, value, result)
    prob_ref[...] = result

    def ring_done(k, carry):
        for c in range(3):
            for way in (0, 1):
                hop(way, k, c).wait_send()
        return carry

    lax.fori_loop(1, HALF, ring_done, 0)
    for way, c, lo, size in last:
        hop(way, HALF, c, lo, size).wait_send()

    def sends_done(d, carry):
        x_copy(d).wait_send()
        r_copy(d).wait_send()
        return carry

    lax.fori_loop(1, NP, sends_done, 0)


def shards(tokens, cotangent, expert_ids, slots, probs, w_gate, w_up, w_down):
    any_spec = pl.BlockSpec(memory_space=pl.ANY)
    vmem = pl.BlockSpec(memory_space=pltpu.VMEM)
    ring_sems = 2 * (HALF + 1) * 3
    return pl.pallas_call(
        kernel,
        out_shape=(
            jax.ShapeDtypeStruct((TOK, D), BF16),
            jax.ShapeDtypeStruct((TOK, 8), F32),
        ),
        in_specs=[any_spec, any_spec, vmem, vmem, vmem, any_spec, any_spec, vmem],
        out_specs=(vmem, vmem),
        scratch_shapes=[
            pltpu.VMEM((3, D, HID), BF16),
            pltpu.VMEM((TOK, D), BF16),
            pltpu.VMEM((TOK, D), BF16),
            pltpu.VMEM((EXP, 2, 16, QW), BF16),
            pltpu.VMEM((2, NP, 16, QW), BF16),
            pltpu.VMEM((2, NQ, ROWS, QW), BF16),
            pltpu.VMEM((3, ROWS, HID), F32),
            pltpu.VMEM((NQ, ROWS, QW), F32),
            pltpu.VMEM((NP, 16, QW), BF16),
            pltpu.VMEM((NP, 16, QW), BF16),
            pltpu.SemaphoreType.DMA((6,)),
            pltpu.SemaphoreType.DMA((ring_sems,)),
            pltpu.SemaphoreType.DMA((ring_sems,)),
            pltpu.SemaphoreType.DMA((NP,)),
            pltpu.SemaphoreType.DMA((NP,)),
            pltpu.SemaphoreType.DMA((NP,)),
            pltpu.SemaphoreType.DMA((NP,)),
        ],
        compiler_params=pltpu.CompilerParams(
            collective_id=0, has_side_effects=True, vmem_limit_bytes=56 * 1024 * 1024
        ),
    )(tokens, cotangent, expert_ids, slots, probs, w_gate, w_up, w_down)


def solution(mesh):
    rows = P(("wide", "narrow"), None)
    in_specs = (rows, rows, rows, rows, rows, P("wide", "narrow"), P("wide", "narrow"), P("narrow", "wide"))
    return jax.shard_map(shards, mesh=mesh, in_specs=in_specs, out_specs=(rows, rows), check_vma=False)
```

time: 489 us -> 112 us (0.23)
  waiting for transfers between devices: 381 us -> 0 us
  Pallas kernels: 0 us -> 103 us
  starting transfers between devices: 53.3 us -> 0 us
  local copies, waits for them, and re-layouts: 26.1 us -> 7.24 us
  between operations: 14.1 us -> 0.65 us
  matrix products: 12.1 us -> 0 us
    all_gather x3 -> x0, waiting for transfers between devices: 320 us -> none  [the longest x1 131 us: shards(): lax.all_gather(w_up, 'wide', axis=0, tiled=True)]
    pallas_call x0 -> x1, Pallas kernels: none -> 103 us  [shards(): pl.pallas_call(kernel, out_shape=(jax.ShapeDtypeStruct((TOK, D), BF16), j...]
    all_to_all x4 -> x0, waiting for transfers between devices: 58.5 us -> none  [the longest x1 15.3 us: shards(): lax.all_to_all(fan_blocks(pick_x), 'narrow', split_axis=0, concat_axis=0,...]
    all_to_all x4 -> x0, starting transfers between devices: 53.2 us -> none  [the longest x1 27.5 us: shards(): lax.all_to_all(part_dx.reshape(narrow_count, CAP, model_width), 'narrow',...]
    dot_general x8 -> x0, matrix products: 12.1 us -> none  [the longest x3 3.29 us: contract_last(): lax.dot_general(left, right, (((1,), (1,)), ((), ())), preferred_element_...]
    scatter x2 -> x0, local copies, waits for them, and re-layouts: 8.61 us -> none  [the longest x1 4.3 us: shards(): source = jnp.full((lanes,), tok_count, jnp.int32).at[target.reshape(-1)]....]
    gather x7 -> x0, local copies, waits for them, and re-layouts: 8.57 us -> none  [the longest x5 7.36 us: shards(): jnp.take_along_axis(scores, jnp.minimum(target, lanes - 1), 1)]
    unnamed x16 -> x11, local copies, waits for them, and re-layouts: 0.84 us -> 5.74 us
  transfers between devices with their start and end apart: 7 -> 0, of which waited for: 7 -> 0; matrix products, arithmetic and copies ran while one was open for 5% -> 0% of each run, Pallas kernels for 0% -> 0%
where the time goes in v1:
time: 112 us; the launch traced here: 111 us
  Pallas kernels  103 us (92%)
  local copies, waits for them, and re-layouts  7.24 us (6%)
    pallas_call x1, Pallas kernels, shards(): pl.pallas_call(kernel, out_shape=(jax.ShapeDtypeStruct((TOK, D), BF16), j...  103 us
    unnamed x11, local copies, waits for them, and re-layouts  5.74 us

profile of v1, /device:TPU:1, one launch (start us, length us, event | category | flops | bytes accessed | tf_op | source)
XLA Modules:
  0.0 111.4 jit_solution(6529997750791884882)
XLA Ops:
  0.6 0.0 copy-start.1
  0.6 1.4 %copy.12.probs_ref = bf16[128,8]{1,0:T(8,128)(2,1)} copy(bf16[128,8]{0,1:T(8,128)(2,1)} %param.12) | data formatting | bytes 4096 | tf_op args[4]
  2.0 0.0 copy-done.1
  2.0 0.0 copy-start.2
  2.0 0.0 copy-start
  2.0 0.7 copy.10.ids_ref
  2.8 0.0 copy-done.2
  2.8 0.7 copy.11.slots_ref
  3.5 0.0 copy-done
  3.5 0.7 copy.13.wd_ref
  4.2 103.5 %shard_map.95 = (bf16[128,3584]{1,0:T(8,128)(2,1)}, f32[128,8]{1,0:T(8,128)}) custom-call(bf16[128,3584]{1,0:T(8,128)(2,1)} %tok_hbm.1, bf16[128,3584]{1,0:T(8,128)(2,1)} %cot_hbm.1, s32[128,8]{1,0:T(8,128)} %copy.10.ids_ref, s32[128,8]{1,0:T(8,128)} %copy.11.slots_ref, bf16[128,8]{1,0:T(8,128)(2,1)} %copy.12.probs_ref, bf16[112,256]{1,0:T(8,128)(2,1)} %wg_hbm.1, ...), custom_call_target="tpu_custom_call" | custom-call | tf_op jit(solution)/shard_map/pallas_call | solution.py:359
  107.7 1.5 %copy.14 = f32[128,8]{0,1:T(8,128)} copy(f32[128,8]{1,0:T(8,128)} %get-tuple-element.3) | data formatting | bytes 8192 | tf_op jit(solution)/shard_map/pallas_call | solution.py:359
  109.2 2.2 %copy.16 = bf16[128,3584]{1,0:T(8,128)(2,1)} copy(bf16[128,3584]{1,0:T(8,128)(2,1)} %get-tuple-element.6) | data formatting | bytes 1835008
Async XLA Ops:
  0.6 1.4 %copy-start.1 = (s32[128,8]{0,1:T(8,128)S(1)}, s32[128,8]{0,1:T(8,128)}, u32[]{:S(2)}) copy-start(s32[128,8]{0,1:T(8,128)} %param.10) | copy-start | bytes 12292
  2.0 0.7 copy-start.2
  2.0 1.5 %copy-start = (bf16[256,112]{0,1:T(8,128)(2,1)S(1)}, bf16[256,112]{0,1:T(8,128)(2,1)}, u32[]{:S(2)}) copy-start(bf16[256,112]{0,1:T(8,128)(2,1)} %param.15) | copy-start | bytes 172036

commit v2 on v1

v2 whole, which is shorter than its diff:
```python
import functools

import jax
import jax.numpy as jnp
from jax import lax
from jax.experimental import pallas as pl
from jax.experimental.pallas import tpu as pltpu
from jax.sharding import PartitionSpec as P

MESH = pl.DeviceIdType.MESH
F32 = jnp.float32
BF16 = jnp.bfloat16

NZ = 32
NP = 32
EXP = 4
PER_EXP = 8
TOK = 128
D = 3584
HID = 256
SH = 112
NQ = 4
QW = D // NQ
LANES = NP * 8
ROWS = NP * 4
HALF = NZ // 2
TURNS = ((0, 0), (1, 2), (0, 1), (1, 1), (0, 2), (1, 0))
CUTS = ((0, 512), (512, 384))


def place(n):
    return lax.rem(n, 2) * (NP // 2) + n // 2


def target_of(ids_ref, slots_ref):
    ids = ids_ref[...]
    return jnp.where(ids < EXP, ids * 4 + slots_ref[...], -1)


def one_hot(target, code, value=None):
    total = jnp.zeros(code.shape, F32)
    for k in range(8):
        held = 1.0 if value is None else value[k : k + 1]
        total = total + jnp.where(target[k : k + 1] == code, held, 0.0)
    return total


def kernel(
    tok_hbm, cot_hbm, ids_ref, slots_ref, probs_ref, wg_hbm, wu_hbm, wd_hbm,
    rin_a, rin_b, spread_ref,
    wbuf, tok, cot, msg, xin, xq, acc, dxs, give_a, give_b, took_a, took_b, out_a, out_b,
    loc_sem, ring_send, ring_recv, x_send, x_recv, c_send, c_recv, r_send, r_recv, word,
):
    w = lax.axis_index("wide")
    n = lax.axis_index("narrow")
    right, left = lax.rem(w + 1, NZ), lax.rem(w + NZ - 1, NZ)
    my_place = place(n)
    my_exp = n // PER_EXP

    def load(i, src, dst):
        return pltpu.make_async_copy(src, dst, loc_sem.at[i])

    def rows_of(shard):
        return pl.ds(pl.multiple_of(shard * SH, 16), SH)

    loads = [
        load(0, wg_hbm, wbuf.at[0, rows_of(w)]),
        load(1, wu_hbm, wbuf.at[1, rows_of(w)]),
        load(6, wd_hbm, wbuf.at[2, rows_of(w)]),
        load(2, tok_hbm, tok),
        load(3, cot_hbm, cot),
    ]
    for one in loads:
        one.start()

    core, chip = lax.rem(n, 2), n // 2
    side = 4 * (chip // 4)
    sibling = chip * 2 + 1 - core
    beside = [(side + lax.rem(chip + d, 4)) * 2 + core for d in (1, 3)]
    above = [lax.rem(chip + d, NP // 2) * 2 + core for d in (4, 12)]
    barrier = pltpu.get_barrier_semaphore()
    for to in [(left, n), (right, n), (w, sibling)] + [(w, one) for one in beside + above]:
        pl.semaphore_signal(barrier, inc=1, device_id=to, device_id_type=MESH)
    pl.semaphore_wait(barrier, 7)

    def tell(i, whom):
        for one in whom:
            pl.semaphore_signal(word.at[i], inc=1, device_id=(w, one), device_id_type=MESH)

    def hear(i, whom):
        pl.semaphore_wait(word.at[i], len(whom))

    tell(0, beside)

    def sem_at(way, k, c):
        return (way * (HALF + 1) + k) * 3 + c

    def hop(way, k, c, lo=0, size=SH, src=None):
        if way == 0:
            shard, to = lax.rem(w + NZ + 1 - k, NZ), right
        else:
            shard, to = lax.rem(w + NZ - 1 + k, NZ), left
        span = pl.ds(pl.multiple_of(shard * SH + lo, 16), size)
        here = wbuf.at[c, span]
        return pltpu.make_async_remote_copy(
            src_ref=here if src is None else src,
            dst_ref=here,
            send_sem=ring_send.at[sem_at(way, k, c)],
            recv_sem=ring_recv.at[sem_at(way, k, c)],
            device_id=(to, n),
            device_id_type=MESH,
        )

    def landed(way, k, c, lo=0, size=SH):
        shard = lax.rem(w + NZ - k, NZ) if way == 0 else lax.rem(w + k, NZ)
        here = wbuf.at[c, pl.ds(pl.multiple_of(shard * SH + lo, 16), size)]
        return pltpu.make_async_remote_copy(
            src_ref=here,
            dst_ref=here,
            send_sem=ring_send.at[sem_at(way, k, c)],
            recv_sem=ring_recv.at[sem_at(way, k, c)],
            device_id=(right, n),
            device_id_type=MESH,
        )

    for way, c in TURNS:
        hop(way, 1, c, src=(wg_hbm, wu_hbm, wd_hbm)[c]).start()

    def step(k):
        for way, c in TURNS:
            landed(way, k, c).wait_recv()
            hop(way, k + 1, c).start()

    def sent(k):
        for c in range(3):
            for way in (0, 1):
                hop(way, k, c).wait_send()

    def steps(lo, hi, more=None):
        def body(k, carry):
            step(k)
            if lo >= 2:
                sent(k - 1)
            if more is not None:
                more(k)
            return carry

        lax.fori_loop(lo, hi, body, 0)

    target = target_of(ids_ref, slots_ref)
    row = lax.broadcasted_iota(jnp.int32, (64, TOK), 0)
    picks = one_hot(target, (row // 16) * 4 + lax.rem(row, 4)).astype(BF16)
    row_q = lax.rem(lax.broadcasted_iota(jnp.int32, (64, QW), 0) // 4, NQ)

    def pick_rows(a, src):
        rows = jnp.zeros((64, QW), F32)
        for q in range(NQ):
            part = jnp.dot(picks, src[:, q * QW : (q + 1) * QW], preferred_element_type=F32)
            rows = jnp.where(row_q == q, part, rows)
        for e in range(EXP):
            msg[e, a] = rows[e * 16 : (e + 1) * 16].astype(BF16)

    def x_copy(d):
        dest = lax.rem(n + d, NP)
        return pltpu.make_async_remote_copy(
            src_ref=msg.at[dest // PER_EXP],
            dst_ref=xin.at[:, my_place],
            send_sem=x_send.at[d],
            recv_sem=x_recv.at[my_place],
            device_id=(w, dest),
            device_id_type=MESH,
        )

    def x_landed(d):
        origin = place(lax.rem(n + d, NP))
        return pltpu.make_async_remote_copy(
            src_ref=msg.at[0],
            dst_ref=xin.at[:, origin],
            send_sem=x_send.at[d],
            recv_sem=x_recv.at[origin],
            device_id=(w, n),
            device_id_type=MESH,
        )

    def x_start(d, carry):
        x_copy(d).start()
        return carry

    loads[3].wait()
    pick_rows(0, tok)
    hear(0, beside)
    tell(1, beside)
    steps(1, 2)
    hear(1, beside)
    tell(2, above)
    loads[4].wait()
    pick_rows(1, cot)
    hear(2, above)
    tell(3, [sibling])
    steps(2, 3)
    hear(3, [sibling])
    lax.fori_loop(1, 11, x_start, 0)
    steps(3, 4)
    lax.fori_loop(11, 21, x_start, 0)
    steps(4, 5)
    lax.fori_loop(21, NP, x_start, 0)
    own_x = load(4, msg.at[my_exp], xin.at[:, my_place])
    own_x.start()
    steps(5, 6)
    row = lax.broadcasted_iota(jnp.int32, (LANES, TOK), 0)
    spread_ref[...] = jnp.transpose(
        one_hot(target, (row // 64) * 4 + lax.rem(row, 4), probs_ref[...].astype(F32))
    ).astype(BF16)
    acc[...] = jnp.zeros_like(acc)
    own_x.wait()
    for one in loads[:3]:
        one.wait()
    steps(6, 9)

    def x_done(d, carry):
        x_copy(d).wait_send()
        return carry

    lax.fori_loop(1, NP, x_done, 0)

    def x_wait(d, carry):
        x_landed(d).wait_recv()
        return carry

    lax.fori_loop(1, NP, x_wait, 0)

    low = lax.broadcasted_iota(jnp.int32, (8, QW), 0) < 4

    def sort_rows(unit):
        a, g = unit // 8, lax.rem(unit, 8)
        block = [xin[a, 4 * g + i].astype(F32) for i in range(4)]
        for half in range(2):
            v = [one[half * 8 : half * 8 + 8] for one in block]
            r = [pltpu.roll(one, 4, 0) for one in v]
            even = [jnp.where(low, v[0], r[1]), jnp.where(low, v[2], r[3])]
            odd = [jnp.where(low, r[0], v[1]), jnp.where(low, r[2], v[3])]
            span = pl.ds(pl.multiple_of(g * 16, 16), 16)
            xq[a, 2 * half, span, :] = jnp.concatenate(even, 0).astype(BF16)
            xq[a, 2 * half + 1, span, :] = jnp.concatenate(odd, 0).astype(BF16)

    def sort_some(k):
        for i in range(4):
            sort_rows((k - 9) * 4 + i)

    steps(9, 13, sort_some)

    def group(j):
        span = pl.ds(pl.multiple_of(j * QW, 16), QW)
        for c in range(3):
            acc[c] += jnp.dot(xq[c // 2, j], wbuf[c, span, :], preferred_element_type=F32)

    j, r = w // 8, lax.rem(w, 8)
    near = lax.rem(j + jnp.where(r <= 3, 3, 1), 4)
    far = lax.rem(j + jnp.where(r <= 3, 1, 3), 4)
    group(j)
    steps(13, 14)
    group(near)
    steps(14, 15)
    last = ((0, 0, 0, SH), (1, 2, 0, SH), (0, 1, 0, 64), (1, 1, 64, 48))
    for way, c in TURNS:
        landed(way, HALF - 1, c).wait_recv()
        for way_l, c_l, lo, size in last:
            if (way_l, c_l) == (way, c):
                hop(way, HALF, c, lo, size).start()
    group(far)
    for way, c, lo, size in last:
        landed(way, HALF, c, lo, size).wait_recv()
    group(lax.rem(j + 2, 4))

    gate, up, raw = acc[0], acc[1], acc[2]
    sigma = 1.0 / (1.0 + jnp.exp(-gate))
    act = gate * sigma
    slope = sigma * (1.0 + gate * (1.0 - sigma))
    d_gate = (raw * up * slope).astype(BF16)
    d_up = (raw * act).astype(BF16)
    score = jnp.sum(act * up * raw, axis=1, keepdims=True)

    row = lax.broadcasted_iota(jnp.int32, (ROWS, 128), 0)
    col = lax.broadcasted_iota(jnp.int32, (ROWS, 128), 1)
    slot = lax.rem(row, 4)
    high = score.astype(BF16).astype(F32)
    marks = jnp.where(col == slot, high, 0.0) + jnp.where(col == slot + 8, score - high, 0.0)
    marks = marks + pltpu.roll(marks, 1, 0)
    marks = marks + pltpu.roll(marks, 2, 0)
    marks = jnp.where(slot == 3, marks, 0.0)

    mine = pl.multiple_of(core * 64, 64)
    other = pl.multiple_of((1 - core) * 64, 64)
    gives, tooks, outs, rins = (give_a, give_b), (took_a, took_b), (out_a, out_b), (rin_a, rin_b)

    def c_copy(h):
        return pltpu.make_async_remote_copy(
            src_ref=gives[h],
            dst_ref=tooks[h],
            send_sem=c_send.at[h],
            recv_sem=c_recv.at[h],
            device_id=(w, sibling),
            device_id_type=MESH,
        )

    nt = (((1,), (1,)), ((), ()))
    for h, (lo, size) in enumerate(CUTS):
        for q in range(NQ):
            span = pl.ds(q * QW + lo, size)
            dxs[q, :, lo : lo + size] = lax.dot_general(
                d_gate, wbuf[0, span, :], nt, preferred_element_type=F32
            ) + lax.dot_general(d_up, wbuf[1, span, :], nt, preferred_element_type=F32)
            if q == 0 and h == 0:
                dxs[0, :, 0:128] += marks
            gives[h][q] = dxs[q, pl.ds(other, 64), lo : lo + size].astype(BF16)
        c_copy(h).start()

    def r_copy(h, dest):
        return pltpu.make_async_remote_copy(
            src_ref=outs[h].at[dest],
            dst_ref=rins[h].at[chip],
            send_sem=r_send.at[h * 16 + dest],
            recv_sem=r_recv.at[h * 16 + chip],
            device_id=(w, dest * 2 + core),
            device_id_type=MESH,
        )

    def r_landed(h, origin):
        return pltpu.make_async_remote_copy(
            src_ref=outs[h].at[0],
            dst_ref=rins[h].at[origin],
            send_sem=r_send.at[h * 16 + origin],
            recv_sem=r_recv.at[h * 16 + origin],
            device_id=(w, n),
            device_id_type=MESH,
        )

    own_r = [load(5 + 2 * h, outs[h].at[chip], rins[h].at[chip]) for h in range(2)]
    mark_rows = (lax.broadcasted_iota(jnp.int32, (8, 128), 0) % 4) == 3
    for h, (lo, size) in enumerate(CUTS):
        c_copy(h).wait_recv()
        low = lax.broadcasted_iota(jnp.int32, (8, size), 0) < 4
        for turn in range(4):
            g = lax.rem(my_exp + turn, 4)
            for i in range(2):
                here = pl.ds(pl.multiple_of(mine + g * 16 + i * 8, 8), 8)
                there = pl.ds(pl.multiple_of(g * 16, 16), 16)
                v = [
                    dxs[q, here, lo : lo + size] + tooks[h][q, there, :].astype(F32)[i * 8 : i * 8 + 8]
                    for q in range(NQ)
                ]
                if h == 0:
                    head = v[0][:, 0:128]
                    rest = head - head.astype(BF16).astype(F32)
                    head = head + jnp.where(mark_rows, pltpu.roll(rest, 8, 1), 0.0)
                    v[0] = jnp.concatenate([head, v[0][:, 128:]], 1)
                r = [pltpu.roll(one, 4, 0) for one in v]
                first = [jnp.where(low, v[0], r[1]), jnp.where(low, v[2], r[3])]
                second = [jnp.where(low, r[0], v[1]), jnp.where(low, r[2], v[3])]
                outs[h][4 * g + 2 * i] = jnp.concatenate(first, 0).astype(BF16)
                outs[h][4 * g + 2 * i + 1] = jnp.concatenate(second, 0).astype(BF16)
            for i in range(4):
                dest = 4 * g + lax.rem(chip + i, 4)
                if turn == 0 and i == 0:
                    own_r[h].start()
                else:
                    r_copy(h, dest).start()

    sent(HALF - 2)
    sent(HALF - 1)
    for way, c, lo, size in last:
        hop(way, HALF, c, lo, size).wait_send()
    for h in range(2):
        c_copy(h).wait_send()
        own_r[h].wait()

    def r_wait(d, carry):
        for h in range(2):
            r_landed(h, lax.rem(chip + d, NP // 2)).wait_recv()
        return carry

    lax.fori_loop(1, NP // 2, r_wait, 0)

    def r_done(d, carry):
        for h in range(2):
            r_copy(h, lax.rem(chip + d, NP // 2)).wait_send()
        return carry

    lax.fori_loop(1, NP // 2, r_done, 0)


def combine(rin_a, rin_b, spread_ref, ids_ref, slots_ref, grad_ref, prob_ref):
    spread = spread_ref[...].astype(F32)
    lane_q = lax.rem(lax.broadcasted_iota(jnp.int32, (TOK, LANES), 1) // 4, NQ)
    mixes = [jnp.where(lane_q == q, spread, 0.0).astype(BF16) for q in range(NQ)]
    for ref, (lo, size) in ((rin_a, CUTS[0]), (rin_b, CUTS[1])):
        rows = ref[...].reshape(LANES, size)
        for q in range(NQ):
            grad_ref[:, q * QW + lo : q * QW + lo + size] = jnp.dot(
                mixes[q], rows, preferred_element_type=F32
            ).astype(BF16)
    rows = rin_a[:, :, 0:128].reshape(LANES, 128)

    s_row = lax.broadcasted_iota(jnp.int32, (16, LANES), 0)
    s_col = lax.broadcasted_iota(jnp.int32, (16, LANES), 1)
    take = (lax.rem(s_col, 16) == 3) & (s_col // 64 == s_row)
    sums = jnp.dot(jnp.where(take, 1.0, 0.0).astype(BF16), rows, preferred_element_type=F32)
    target = target_of(ids_ref, slots_ref)
    result = jnp.zeros((8, TOK), F32)
    for e in range(EXP):
        for s in range(3):
            value = sums[e : e + 1, s : s + 1] + sums[e : e + 1, s + 8 : s + 9]
            result = jnp.where(target == e * 4 + s, value, result)
    prob_ref[...] = result


def shards(tokens, cotangent, expert_ids, slots, probs, w_gate, w_up, w_down):
    any_spec = pl.BlockSpec(memory_space=pl.ANY)
    vmem = pl.BlockSpec(memory_space=pltpu.VMEM)
    ring_sems = 2 * (HALF + 1) * 3
    ids_t, slots_t = expert_ids.T, slots.T
    rins_a, rins_b, spread = pl.pallas_call(
        kernel,
        out_shape=(
            jax.ShapeDtypeStruct((NP // 2, 16, CUTS[0][1]), BF16),
            jax.ShapeDtypeStruct((NP // 2, 16, CUTS[1][1]), BF16),
            jax.ShapeDtypeStruct((TOK, LANES), BF16),
        ),
        in_specs=[any_spec, any_spec, vmem, vmem, vmem, any_spec, any_spec, any_spec],
        out_specs=(any_spec, any_spec, vmem),
        scratch_shapes=[
            pltpu.VMEM((3, D, HID), BF16),
            pltpu.VMEM((TOK, D), BF16),
            pltpu.VMEM((TOK, D), BF16),
            pltpu.VMEM((EXP, 2, 16, QW), BF16),
            pltpu.VMEM((2, NP, 16, QW), BF16),
            pltpu.VMEM((2, NQ, ROWS, QW), BF16),
            pltpu.VMEM((3, ROWS, HID), F32),
            pltpu.VMEM((NQ, ROWS, QW), F32),
            pltpu.VMEM((NQ, ROWS // 2, CUTS[0][1]), BF16),
            pltpu.VMEM((NQ, ROWS // 2, CUTS[1][1]), BF16),
            pltpu.VMEM((NQ, ROWS // 2, CUTS[0][1]), BF16),
            pltpu.VMEM((NQ, ROWS // 2, CUTS[1][1]), BF16),
            pltpu.VMEM((NP // 2, 16, CUTS[0][1]), BF16),
            pltpu.VMEM((NP // 2, 16, CUTS[1][1]), BF16),
            pltpu.SemaphoreType.DMA((8,)),
            pltpu.SemaphoreType.DMA((ring_sems,)),
            pltpu.SemaphoreType.DMA((ring_sems,)),
            pltpu.SemaphoreType.DMA((NP,)),
            pltpu.SemaphoreType.DMA((NP,)),
            pltpu.SemaphoreType.DMA((2,)),
            pltpu.SemaphoreType.DMA((2,)),
            pltpu.SemaphoreType.DMA((NP,)),
            pltpu.SemaphoreType.DMA((NP,)),
            pltpu.SemaphoreType.REGULAR((4,)),
        ],
        compiler_params=pltpu.CompilerParams(
            collective_id=0, has_side_effects=True, vmem_limit_bytes=56 * 1024 * 1024
        ),
    )(tokens, cotangent, ids_t, slots_t, probs.T, w_gate, w_up, w_down.T)
    grad, prob_t = pl.pallas_call(
        combine,
        out_shape=(jax.ShapeDtypeStruct((TOK, D), BF16), jax.ShapeDtypeStruct((8, TOK), F32)),
        in_specs=[vmem] * 5,
        out_specs=(vmem, vmem),
    )(rins_a, rins_b, spread, ids_t, slots_t)
    return grad, prob_t.T


def solution(mesh):
    rows = P(("wide", "narrow"), None)
    in_specs = (rows, rows, rows, rows, rows, P("wide", "narrow"), P("wide", "narrow"), P("narrow", "wide"))
    return jax.shard_map(shards, mesh=mesh, in_specs=in_specs, out_specs=(rows, rows), check_vma=False)
```

time: 112 us -> 105 us (0.938)
  local copies, waits for them, and re-layouts: 7.24 us -> 0 us
    unnamed x11 -> x0, local copies, waits for them, and re-layouts: 5.74 us -> none
    pallas_call x1 -> x0, local copies, waits for them, and re-layouts: 1.5 us -> none  [shards(): pl.pallas_call(kernel, out_shape=(jax.ShapeDtypeStruct((TOK, D), BF16), j...]
    pallas_call x1 -> x2, Pallas kernels: 103 us -> 104 us  [the longest x1 101 us: shards(): pl.pallas_call(kernel, out_shape=(jax.ShapeDtypeStruct((NP // 2, 16, CUTS...]
where the time goes in v2:
time: 105 us
  Pallas kernels  104 us (99%)
    pallas_call x1, Pallas kernels, shards(): pl.pallas_call(kernel, out_shape=(jax.ShapeDtypeStruct((NP // 2, 16, CUTS...  101 us
    pallas_call x1, Pallas kernels, shards(): pl.pallas_call(combine, out_shape=(jax.ShapeDtypeStruct((TOK, D), BF16),...  2.53 us

profile of v2, /device:TPU:1, one launch (start us, length us, event | category | flops | bytes accessed | tf_op | source)
XLA Modules:
  0.0 104.6 jit_solution(13478833903156706640)
XLA Ops:
  0.6 101.5 %shard_map.95 = (bf16[16,16,512]{2,1,0:T(8,128)(2,1)}, bf16[16,16,384]{2,1,0:T(8,128)(2,1)}, bf16[128,256]{1,0:T(8,128)(2,1)}) custom-call(bf16[128,3584]{1,0:T(8,128)(2,1)} %tok_hbm.1, bf16[128,3584]{1,0:T(8,128)(2,1)} %cot_hbm.1, s32[8,128]{1,0:T(8,128)} %bitcast.6, s32[8,128]{1,0:T(8,128)} %bitcast.8, bf16[8,128]{1,0:T(8,128)(2,1)} %bitcast.10, ...), custom_call_target="tpu_custom_call" | custom-call | tf_op jit(solution)/shard_map/pallas_call | solution.py:422
  102.1 2.5 %shard_map.96 = (bf16[128,3584]{1,0:T(8,128)(2,1)}, f32[8,128]{1,0:T(8,128)}) custom-call(bf16[16,16,512]{2,1,0:T(8,128)(2,1)} %get-tuple-element.7.rin_a, bf16[16,16,384]{2,1,0:T(8,128)(2,1)} %get-tuple-element.8.rin_b, bf16[128,256]{1,0:T(8,128)(2,1)} %get-tuple-element.9.spread_ref, s32[8,128]{1,0:T(8,128)} %bitcast.7, s32[8,128]{1,0:T(8,128)} %bitcast.9), custom_call_target="tpu_custom_call" | custom-call | tf_op jit(solution)/shard_map/pallas_call | solution.py:461

commit v3 on v2

--- a/solution.py
+++ b/solution.py
@@ -24,12 +24,17 @@
 LANES = NP * 8
 ROWS = NP * 4
 HALF = NZ // 2
-TURNS = ((0, 0), (1, 2), (0, 1), (1, 1), (0, 2), (1, 0))
+FAR_FIRST = (2, 1, 3, 0)
+MOST = HALF + 2
 CUTS = ((0, 512), (512, 384))
 
 
 def place(n):
     return lax.rem(n, 2) * (NP // 2) + n // 2
+
+
+def lean(z):
+    return jnp.where(z < 5, 1, 0)
 
 
 def target_of(ids_ref, slots_ref):
@@ -46,14 +51,15 @@
 
 
 def kernel(
-    tok_hbm, cot_hbm, ids_ref, slots_ref, probs_ref, wg_hbm, wu_hbm, wd_hbm,
-    rin_a, rin_b, spread_ref,
-    wbuf, tok, cot, msg, xin, xq, acc, dxs, give_a, give_b, took_a, took_b, out_a, out_b,
-    loc_sem, ring_send, ring_recv, x_send, x_recv, c_send, c_recv, r_send, r_recv, word,
+    tok_hbm, cot_hbm, ids_hbm, slots_hbm, probs_hbm, wg_hbm, wu_hbm, wd_hbm,
+    rin_a, rin_b, spread_hbm,
+    ids_ref, slots_ref, probs_ref, spread_ref, wbuf, tok, cot, msg, xin, xq, acc, dxs, give_a, give_b, took_a, took_b, out_a, out_b,
+    loc_sem, ring_send, ring_recv, cross_send, cross_recv, x_send, x_recv, c_send, c_recv, r_send, r_recv, word,
 ):
     w = lax.axis_index("wide")
     n = lax.axis_index("narrow")
     right, left = lax.rem(w + 1, NZ), lax.rem(w + NZ - 1, NZ)
+    core, chip = lax.rem(n, 2), n // 2
     my_place = place(n)
     my_exp = n // PER_EXP
 
@@ -64,24 +70,26 @@
         return pl.ds(pl.multiple_of(shard * SH, 16), SH)
 
     loads = [
-        load(0, wg_hbm, wbuf.at[0, rows_of(w)]),
-        load(1, wu_hbm, wbuf.at[1, rows_of(w)]),
-        load(6, wd_hbm, wbuf.at[2, rows_of(w)]),
+        load(0, wg_hbm, wbuf.at[core, 0, rows_of(w)]),
+        load(1, wu_hbm, wbuf.at[core, 1, rows_of(w)]),
+        load(6, wd_hbm, wbuf.at[core, 2, rows_of(w)]),
         load(2, tok_hbm, tok),
         load(3, cot_hbm, cot),
+        load(8, ids_hbm, ids_ref),
+        load(9, slots_hbm, slots_ref),
+        load(10, probs_hbm, probs_ref),
     ]
     for one in loads:
         one.start()
 
-    core, chip = lax.rem(n, 2), n // 2
     side = 4 * (chip // 4)
     sibling = chip * 2 + 1 - core
     beside = [(side + lax.rem(chip + d, 4)) * 2 + core for d in (1, 3)]
     above = [lax.rem(chip + d, NP // 2) * 2 + core for d in (4, 12)]
     barrier = pltpu.get_barrier_semaphore()
-    for to in [(left, n), (right, n), (w, sibling)] + [(w, one) for one in beside + above]:
+    for to in [(z, chip * 2 + i) for z in (left, right) for i in (0, 1)] + [(w, sibling)] + [(w, one) for one in beside + above]:
         pl.semaphore_signal(barrier, inc=1, device_id=to, device_id_type=MESH)
-    pl.semaphore_wait(barrier, 7)
+    pl.semaphore_wait(barrier, 9)
 
     def tell(i, whom):
         for one in whom:
@@ -92,61 +100,118 @@
 
     tell(0, beside)
 
-    def sem_at(way, k, c):
-        return (way * (HALF + 1) + k) * 3 + c
-
-    def hop(way, k, c, lo=0, size=SH, src=None):
-        if way == 0:
-            shard, to = lax.rem(w + NZ + 1 - k, NZ), right
-        else:
-            shard, to = lax.rem(w + NZ - 1 + k, NZ), left
-        span = pl.ds(pl.multiple_of(shard * SH + lo, 16), size)
-        here = wbuf.at[c, span]
-        return pltpu.make_async_remote_copy(
-            src_ref=here if src is None else src,
-            dst_ref=here,
-            send_sem=ring_send.at[sem_at(way, k, c)],
-            recv_sem=ring_recv.at[sem_at(way, k, c)],
-            device_id=(to, n),
-            device_id_type=MESH,
-        )
-
-    def landed(way, k, c, lo=0, size=SH):
-        shard = lax.rem(w + NZ - k, NZ) if way == 0 else lax.rem(w + k, NZ)
-        here = wbuf.at[c, pl.ds(pl.multiple_of(shard * SH + lo, 16), size)]
+    onward = jnp.where(core == 0, right, left)
+    reach = jnp.where(core == 0, HALF - 1 - lean(w), HALF - 1 + lean(w))
+    reach_next = jnp.where(core == 0, HALF - 1 - lean(onward), HALF - 1 + lean(onward))
+    reach_other = jnp.where(core == 0, HALF - 1 + lean(w), HALF - 1 - lean(w))
+    extra = (1, 1 - core, 0)
+    extra_other = (1, core, 0)
+
+    def weight(j, way):
+        return j + way * (2 - 2 * j)
+
+    def shard_at(k, way):
+        return jnp.where(way == 0, lax.rem(w + NZ - k, NZ), lax.rem(w + k, NZ))
+
+    def sem_at(k, o, j):
+        return (k * 2 + o) * 3 + j
+
+    def first_hop(way, c):
+        j = weight(c, way)
+        return pltpu.make_async_remote_copy(
+            src_ref=(wg_hbm, wu_hbm, wd_hbm)[c],
+            dst_ref=wbuf.at[core, c, rows_of(w)],
+            send_sem=ring_send.at[sem_at(0, way, j)],
+            recv_sem=ring_recv.at[sem_at(1, core, j)],
+            device_id=((right, left)[way], chip * 2 + way),
+            device_id_type=MESH,
+        )
+
+    def hop(k, o, j):
+        here = wbuf.at[o, weight(j, core), rows_of(shard_at(k, core))]
         return pltpu.make_async_remote_copy(
             src_ref=here,
             dst_ref=here,
-            send_sem=ring_send.at[sem_at(way, k, c)],
-            recv_sem=ring_recv.at[sem_at(way, k, c)],
-            device_id=(right, n),
-            device_id_type=MESH,
-        )
-
-    for way, c in TURNS:
-        hop(way, 1, c, src=(wg_hbm, wu_hbm, wd_hbm)[c]).start()
+            send_sem=ring_send.at[sem_at(k, o, j)],
+            recv_sem=ring_recv.at[sem_at(k + 1, o, j)],
+            device_id=(onward, n),
+            device_id_type=MESH,
+        )
+
+    def landed(k, o, j):
+        here = wbuf.at[o, weight(j, core), rows_of(shard_at(k, core))]
+        return pltpu.make_async_remote_copy(
+            src_ref=here,
+            dst_ref=here,
+            send_sem=ring_send.at[sem_at(k, o, j)],
+            recv_sem=ring_recv.at[sem_at(k, o, j)],
+            device_id=(onward, n),
+            device_id_type=MESH,
+        )
+
+    def cross(k, j, owner, way):
+        here = wbuf.at[owner, weight(j, way), rows_of(shard_at(k, way))]
+        return pltpu.make_async_remote_copy(
+            src_ref=here,
+            dst_ref=here,
+            send_sem=cross_send.at[k * 3 + j],
+            recv_sem=cross_recv.at[k * 3 + j],
+            device_id=(w, sibling),
+            device_id_type=MESH,
+        )
+
+    for i in range(3):
+        for way in (0, 1):
+            first_hop(way, weight(i, way)).start()
 
     def step(k):
-        for way, c in TURNS:
-            landed(way, k, c).wait_recv()
-            hop(way, k + 1, c).start()
+        for j in range(3):
+
+            @pl.when(k <= reach + extra[j])
+            def _():
+                for o in range(2):
+                    landed(k, o, j).wait_recv()
+
+                    @pl.when(k < reach_next + extra[j])
+                    def _():
+                        hop(k, o, j).start()
+
+                cross(k, j, 1 - core, core).start()
 
     def sent(k):
-        for c in range(3):
-            for way in (0, 1):
-                hop(way, k, c).wait_send()
+        for j in range(3):
+
+            @pl.when(k < reach_next + extra[j])
+            def _():
+                for o in range(2):
+                    hop(k, o, j).wait_send()
+
+            @pl.when(k <= reach + extra[j])
+            def _():
+                cross(k, j, 1 - core, core).wait_send()
+
+    def crossed(k):
+        for j in range(3):
+
+            @pl.when(k <= reach_other + extra_other[j])
+            def _():
+                cross(k, j, core, 1 - core).wait_recv()
 
     def steps(lo, hi, more=None):
         def body(k, carry):
             step(k)
-            if lo >= 2:
-                sent(k - 1)
+            if lo >= 3:
+                sent(k - 2)
+            if lo >= 8:
+                crossed(k - 7)
             if more is not None:
                 more(k)
             return carry
 
         lax.fori_loop(lo, hi, body, 0)
 
+    for one in loads[5:]:
+        one.wait()
     target = target_of(ids_ref, slots_ref)
     row = lax.broadcasted_iota(jnp.int32, (64, TOK), 0)
     picks = one_hot(target, (row // 16) * 4 + lax.rem(row, 4)).astype(BF16)
@@ -190,32 +255,30 @@
     pick_rows(0, tok)
     hear(0, beside)
     tell(1, beside)
-    steps(1, 2)
+    loads[4].wait()
+    pick_rows(1, cot)
     hear(1, beside)
     tell(2, above)
-    loads[4].wait()
-    pick_rows(1, cot)
+    acc[...] = jnp.zeros_like(acc)
     hear(2, above)
     tell(3, [sibling])
-    steps(2, 3)
+    steps(1, 2)
     hear(3, [sibling])
-    lax.fori_loop(1, 11, x_start, 0)
-    steps(3, 4)
-    lax.fori_loop(11, 21, x_start, 0)
-    steps(4, 5)
-    lax.fori_loop(21, NP, x_start, 0)
+    lax.fori_loop(1, NP, x_start, 0)
     own_x = load(4, msg.at[my_exp], xin.at[:, my_place])
     own_x.start()
-    steps(5, 6)
+    steps(2, 3)
     row = lax.broadcasted_iota(jnp.int32, (LANES, TOK), 0)
     spread_ref[...] = jnp.transpose(
         one_hot(target, (row // 64) * 4 + lax.rem(row, 4), probs_ref[...].astype(F32))
     ).astype(BF16)
-    acc[...] = jnp.zeros_like(acc)
+    save = load(11, spread_ref, spread_hbm)
+    save.start()
     own_x.wait()
     for one in loads[:3]:
         one.wait()
-    steps(6, 9)
+    steps(3, 8)
+    steps(8, 12)
 
     def x_done(d, carry):
         x_copy(d).wait_send()
@@ -245,31 +308,27 @@
 
     def sort_some(k):
         for i in range(4):
-            sort_rows((k - 9) * 4 + i)
-
-    steps(9, 13, sort_some)
+            sort_rows((k - 12) * 4 + i)
+
+    save.wait()
+    steps(12, 16, sort_some)
 
     def group(j):
         span = pl.ds(pl.multiple_of(j * QW, 16), QW)
         for c in range(3):
-            acc[c] += jnp.dot(xq[c // 2, j], wbuf[c, span, :], preferred_element_type=F32)
+            acc[c] += jnp.dot(xq[c // 2, j], wbuf[core, c, span, :], preferred_element_type=F32)
 
     j, r = w // 8, lax.rem(w, 8)
     near = lax.rem(j + jnp.where(r <= 3, 3, 1), 4)
     far = lax.rem(j + jnp.where(r <= 3, 1, 3), 4)
     group(j)
-    steps(13, 14)
+    steps(16, MOST + 1)
     group(near)
-    steps(14, 15)
-    last = ((0, 0, 0, SH), (1, 2, 0, SH), (0, 1, 0, 64), (1, 1, 64, 48))
-    for way, c in TURNS:
-        landed(way, HALF - 1, c).wait_recv()
-        for way_l, c_l, lo, size in last:
-            if (way_l, c_l) == (way, c):
-                hop(way, HALF, c, lo, size).start()
+    for k in range(MOST - 6, HALF):
+        crossed(k)
     group(far)
-    for way, c, lo, size in last:
-        landed(way, HALF, c, lo, size).wait_recv()
+    for k in range(HALF, MOST + 1):
+        crossed(k)
     group(lax.rem(j + 2, 4))
 
     gate, up, raw = acc[0], acc[1], acc[2]
@@ -308,8 +367,8 @@
         for q in range(NQ):
             span = pl.ds(q * QW + lo, size)
             dxs[q, :, lo : lo + size] = lax.dot_general(
-                d_gate, wbuf[0, span, :], nt, preferred_element_type=F32
-            ) + lax.dot_general(d_up, wbuf[1, span, :], nt, preferred_element_type=F32)
+                d_gate, wbuf[core, 0, span, :], nt, preferred_element_type=F32
+            ) + lax.dot_general(d_up, wbuf[core, 1, span, :], nt, preferred_element_type=F32)
             if q == 0 and h == 0:
                 dxs[0, :, 0:128] += marks
             gives[h][q] = dxs[q, pl.ds(other, 64), lo : lo + size].astype(BF16)
@@ -340,7 +399,7 @@
     for h, (lo, size) in enumerate(CUTS):
         c_copy(h).wait_recv()
         low = lax.broadcasted_iota(jnp.int32, (8, size), 0) < 4
-        for turn in range(4):
+        for turn in FAR_FIRST:
             g = lax.rem(my_exp + turn, 4)
             for i in range(2):
                 here = pl.ds(pl.multiple_of(mine + g * 16 + i * 8, 8), 8)
@@ -359,20 +418,28 @@
                 second = [jnp.where(low, r[0], v[1]), jnp.where(low, r[2], v[3])]
                 outs[h][4 * g + 2 * i] = jnp.concatenate(first, 0).astype(BF16)
                 outs[h][4 * g + 2 * i + 1] = jnp.concatenate(second, 0).astype(BF16)
-            for i in range(4):
+            for i in FAR_FIRST:
                 dest = 4 * g + lax.rem(chip + i, 4)
                 if turn == 0 and i == 0:
                     own_r[h].start()
                 else:
                     r_copy(h, dest).start()
 
-    sent(HALF - 2)
-    sent(HALF - 1)
-    for way, c, lo, size in last:
-        hop(way, HALF, c, lo, size).wait_send()
+    for way in (0, 1):
+        for c in range(3):
+            first_hop(way, c).wait_send()
+    for k in (MOST - 1, MOST):
+        sent(k)
     for h in range(2):
         c_copy(h).wait_send()
         own_r[h].wait()
+
+    def r_done(d, carry):
+        for h in range(2):
+            r_copy(h, lax.rem(chip + d, NP // 2)).wait_send()
+        return carry
+
+    lax.fori_loop(1, NP // 2, r_done, 0)
 
     def r_wait(d, carry):
         for h in range(2):
@@ -380,13 +447,6 @@
         return carry
 
     lax.fori_loop(1, NP // 2, r_wait, 0)
-
-    def r_done(d, carry):
-        for h in range(2):
-            r_copy(h, lax.rem(chip + d, NP // 2)).wait_send()
-        return carry
-
-    lax.fori_loop(1, NP // 2, r_done, 0)
 
 
 def combine(rin_a, rin_b, spread_ref, ids_ref, slots_ref, grad_ref, prob_ref):
@@ -417,7 +477,7 @@
 def shards(tokens, cotangent, expert_ids, slots, probs, w_gate, w_up, w_down):
     any_spec = pl.BlockSpec(memory_space=pl.ANY)
     vmem = pl.BlockSpec(memory_space=pltpu.VMEM)
-    ring_sems = 2 * (HALF + 1) * 3
+    ring_sems = (MOST + 2) * 6
     ids_t, slots_t = expert_ids.T, slots.T
     rins_a, rins_b, spread = pl.pallas_call(
         kernel,
@@ -426,10 +486,14 @@
             jax.ShapeDtypeStruct((NP // 2, 16, CUTS[1][1]), BF16),
             jax.ShapeDtypeStruct((TOK, LANES), BF16),
         ),
-        in_specs=[any_spec, any_spec, vmem, vmem, vmem, any_spec, any_spec, any_spec],
-        out_specs=(any_spec, any_spec, vmem),
+        in_specs=[any_spec] * 8,
+        out_specs=(any_spec, any_spec, any_spec),
         scratch_shapes=[
-            pltpu.VMEM((3, D, HID), BF16),
+            pltpu.VMEM((8, TOK), jnp.int32),
+            pltpu.VMEM((8, TOK), jnp.int32),
+            pltpu.VMEM((8, TOK), BF16),
+            pltpu.VMEM((TOK, LANES), BF16),
+            pltpu.VMEM((2, 3, D, HID), BF16),
             pltpu.VMEM((TOK, D), BF16),
             pltpu.VMEM((TOK, D), BF16),
             pltpu.VMEM((EXP, 2, 16, QW), BF16),
@@ -443,9 +507,11 @@
             pltpu.VMEM((NQ, ROWS // 2, CUTS[1][1]), BF16),
             pltpu.VMEM((NP // 2, 16, CUTS[0][1]), BF16),
             pltpu.VMEM((NP // 2, 16, CUTS[1][1]), BF16),
-            pltpu.SemaphoreType.DMA((8,)),
+            pltpu.SemaphoreType.DMA((12,)),
             pltpu.SemaphoreType.DMA((ring_sems,)),
             pltpu.SemaphoreType.DMA((ring_sems,)),
+            pltpu.SemaphoreType.DMA((ring_sems // 2,)),
+            pltpu.SemaphoreType.DMA((ring_sems // 2,)),
             pltpu.SemaphoreType.DMA((NP,)),
             pltpu.SemaphoreType.DMA((NP,)),
             pltpu.SemaphoreType.DMA((2,)),

time: 105 us -> 99.4 us (0.947)
  Pallas kernels: 104 us -> 98.6 us
    pallas_call x1, Pallas kernels: 101 us -> 96.1 us  [shards(): pl.pallas_call(kernel, out_shape=(jax.ShapeDtypeStruct((NP // 2, 16, CUTS...]
where the time goes in v3:
time: 99.4 us; the launch traced here: 99.2 us
  Pallas kernels  98.6 us (99%)
    pallas_call x1, Pallas kernels, shards(): pl.pallas_call(kernel, out_shape=(jax.ShapeDtypeStruct((NP // 2, 16, CUTS...  96.1 us
    pallas_call x1, Pallas kernels, shards(): pl.pallas_call(combine, out_shape=(jax.ShapeDtypeStruct((TOK, D), BF16),...  2.53 us

profile of v3, /device:TPU:1, one launch (start us, length us, event | category | flops | bytes accessed | tf_op | source)
XLA Modules:
  0.0 99.2 jit_solution(392028797460505954)
XLA Ops:
  0.6 96.1 %shard_map.95 = (bf16[16,16,512]{2,1,0:T(8,128)(2,1)}, bf16[16,16,384]{2,1,0:T(8,128)(2,1)}, bf16[128,256]{1,0:T(8,128)(2,1)}) custom-call(bf16[128,3584]{1,0:T(8,128)(2,1)} %tok_hbm.1, bf16[128,3584]{1,0:T(8,128)(2,1)} %cot_hbm.1, s32[8,128]{1,0:T(8,128)} %bitcast.6, s32[8,128]{1,0:T(8,128)} %bitcast.8, bf16[8,128]{1,0:T(8,128)(2,1)} %bitcast.10, ...), custom_call_target="tpu_custom_call" | custom-call | tf_op jit(solution)/shard_map/pallas_call | solution.py:482
  96.7 2.5 %shard_map.96 = (bf16[128,3584]{1,0:T(8,128)(2,1)}, f32[8,128]{1,0:T(8,128)}) custom-call(bf16[16,16,512]{2,1,0:T(8,128)(2,1)} %get-tuple-element.7.rin_a, bf16[16,16,384]{2,1,0:T(8,128)(2,1)} %get-tuple-element.8.rin_b, bf16[128,256]{1,0:T(8,128)(2,1)} %get-tuple-element.9.spread_ref, s32[8,128]{1,0:T(8,128)} %bitcast.7, s32[8,128]{1,0:T(8,128)} %bitcast.9), custom_call_target="tpu_custom_call" | custom-call | tf_op jit(solution)/shard_map/pallas_call | solution.py:527

commit v4 on v3

--- a/solution.py
+++ b/solution.py
@@ -202,7 +202,7 @@
             step(k)
             if lo >= 3:
                 sent(k - 2)
-            if lo >= 8:
+            if 8 <= lo < 12:
                 crossed(k - 7)
             if more is not None:
                 more(k)
@@ -262,12 +262,14 @@
     acc[...] = jnp.zeros_like(acc)
     hear(2, above)
     tell(3, [sibling])
+    hear(3, [sibling])
+    lax.fori_loop(1, 11, x_start, 0)
     steps(1, 2)
-    hear(3, [sibling])
-    lax.fori_loop(1, NP, x_start, 0)
+    lax.fori_loop(11, 21, x_start, 0)
+    steps(2, 3)
+    lax.fori_loop(21, NP, x_start, 0)
     own_x = load(4, msg.at[my_exp], xin.at[:, my_place])
     own_x.start()
-    steps(2, 3)
     row = lax.broadcasted_iota(jnp.int32, (LANES, TOK), 0)
     spread_ref[...] = jnp.transpose(
         one_hot(target, (row // 64) * 4 + lax.rem(row, 4), probs_ref[...].astype(F32))
@@ -278,7 +280,7 @@
     for one in loads[:3]:
         one.wait()
     steps(3, 8)
-    steps(8, 12)
+    steps(8, 10)
 
     def x_done(d, carry):
         x_copy(d).wait_send()
@@ -308,10 +310,16 @@
 
     def sort_some(k):
         for i in range(4):
-            sort_rows((k - 12) * 4 + i)
+            sort_rows((k - 10) * 4 + i)
+
+    def hear_some(k):
+        for i in range(2):
+            crossed(5 + (k - 12) * 2 + i)
 
     save.wait()
-    steps(12, 16, sort_some)
+    steps(10, 12, sort_some)
+    steps(12, 14, lambda k: (sort_some(k), hear_some(k)))
+    crossed(9)
 
     def group(j):
         span = pl.ds(pl.multiple_of(j * QW, 16), QW)
@@ -322,9 +330,12 @@
     near = lax.rem(j + jnp.where(r <= 3, 3, 1), 4)
     far = lax.rem(j + jnp.where(r <= 3, 1, 3), 4)
     group(j)
-    steps(16, MOST + 1)
+    steps(14, 15)
+    crossed(10)
+    crossed(11)
     group(near)
-    for k in range(MOST - 6, HALF):
+    steps(15, MOST + 1)
+    for k in range(12, HALF):
         crossed(k)
     group(far)
     for k in range(HALF, MOST + 1):

time: 99.4 us -> 98.6 us (level)
  no operation moved by 1% of the time
where the time goes in v4:
time: 98.6 us; the launch traced here: 98.5 us
  Pallas kernels  97.8 us (99%)
    pallas_call x1, Pallas kernels, shards(): pl.pallas_call(kernel, out_shape=(jax.ShapeDtypeStruct((NP // 2, 16, CUTS...  95.3 us
    pallas_call x1, Pallas kernels, shards(): pl.pallas_call(combine, out_shape=(jax.ShapeDtypeStruct((TOK, D), BF16),...  2.53 us

profile of v4, /device:TPU:1, one launch (start us, length us, event | category | flops | bytes accessed | tf_op | source)
XLA Modules:
  0.0 98.5 jit_solution(9155015288347266992)
XLA Ops:
  0.6 95.3 %shard_map.95 = (bf16[16,16,512]{2,1,0:T(8,128)(2,1)}, bf16[16,16,384]{2,1,0:T(8,128)(2,1)}, bf16[128,256]{1,0:T(8,128)(2,1)}) custom-call(bf16[128,3584]{1,0:T(8,128)(2,1)} %tok_hbm.1, bf16[128,3584]{1,0:T(8,128)(2,1)} %cot_hbm.1, s32[8,128]{1,0:T(8,128)} %bitcast.6, s32[8,128]{1,0:T(8,128)} %bitcast.8, bf16[8,128]{1,0:T(8,128)(2,1)} %bitcast.10, ...), custom_call_target="tpu_custom_call" | custom-call | tf_op jit(solution)/shard_map/pallas_call | solution.py:493
  96.0 2.5 %shard_map.96 = (bf16[128,3584]{1,0:T(8,128)(2,1)}, f32[8,128]{1,0:T(8,128)}) custom-call(bf16[16,16,512]{2,1,0:T(8,128)(2,1)} %get-tuple-element.7.rin_a, bf16[16,16,384]{2,1,0:T(8,128)(2,1)} %get-tuple-element.8.rin_b, bf16[128,256]{1,0:T(8,128)(2,1)} %get-tuple-element.9.spread_ref, s32[8,128]{1,0:T(8,128)} %bitcast.7, s32[8,128]{1,0:T(8,128)} %bitcast.9), custom_call_target="tpu_custom_call" | custom-call | tf_op jit(solution)/shard_map/pallas_call | solution.py:538
